TPU v7x, 1024 devices: a whole 4x4x32 slice. The times are simulated.
1024 devices in a mesh: dp: 32 (over z_lo, y), expert: 32 (over x, z_hi, core).
Axes of the slice: x: 4, y: 4, z: 32 (z_hi: 4, z_lo: 8; z = z_hi * 8 + z_lo), core: 2. Of those that a mesh axis runs over, the one named last changes fastest.
Arguments:
- tokens: bfloat16 [131072, 2048], P(('dp', 'expert')), may hold values from -6 to 6
- expert_ids: int32 [131072, 2], P(('dp', 'expert')), may hold values from 0 to 15, all different within a row
- copy_choice: int32 [131072, 2], P(('dp', 'expert')), may hold values from 0 to 1
- gate_weights: float32 [131072, 2], P(('dp', 'expert')), may hold values from 0.05 to 1
- w_gate: bfloat16 [2048, 24576], P(None, 'expert'), may hold values from -0.125 to 0.125
- w_up: bfloat16 [2048, 24576], P(None, 'expert'), may hold values from -0.125 to 0.125
- w_down: bfloat16 [24576, 2048], P('expert'), may hold values from -0.15625 to 0.15625
Outputs:
- moe_out: bfloat16 [131072, 2048], P(('dp', 'expert'))
- expert_load: float32 [16], replicated
Inputs may be any that keep to these rules, and one draw needn't show every extreme that they name: `expert_ids`: the 2 experts of a token are distinct.
All inputs are finite; a program needn't handle non-finite values.
Results may differ from a plain program's by a relative error of at most 0.0049.
Values may be sent and summed in bfloat16 or wider, within the bound.
A program may use at most 64 MiB of HBM per device.

v0:
```python
import jax
import jax.numpy as jnp
from jax import lax
from jax.sharding import PartitionSpec as P


def expert_pass(inputs, weight_gate, weight_up, weight_down):
    gate_act = jnp.dot(inputs, weight_gate, preferred_element_type=jnp.float32)
    up_act = jnp.dot(inputs, weight_up, preferred_element_type=jnp.float32)
    hidden = (jax.nn.silu(gate_act) * up_act).astype(jnp.bfloat16)
    return jnp.dot(hidden, weight_down, preferred_element_type=jnp.float32)


def local(tokens, expert_ids, copy_choice, gate_weights, w_gate, w_up, w_down):
    members = lax.axis_size("expert")
    experts = members // 2
    tok_rows, chosen = expert_ids.shape
    features = tokens.shape[1]
    capacity = max(2, tok_rows * chosen // (2 * experts))
    sections = 2 * experts
    route_keys = (expert_ids * 2 + copy_choice).reshape(-1)
    onehot = (route_keys[:, None] == jnp.arange(sections, dtype=jnp.int32)[None, :]).astype(
        jnp.int32
    )
    before = jnp.cumsum(onehot, axis=0) - onehot
    slot_rank = jnp.sum(before * onehot, axis=1)
    retained = slot_rank < capacity
    target = jnp.where(retained, route_keys * capacity + slot_rank, -1).reshape(tok_rows, chosen)
    places = jnp.arange(sections * capacity, dtype=jnp.int32)
    matches = places[:, None, None] == target[None, :, :]
    dispatch = jnp.sum(matches.astype(jnp.float32), axis=2).astype(jnp.bfloat16)
    packed = jnp.dot(dispatch, tokens, preferred_element_type=jnp.float32).astype(jnp.bfloat16)
    packed = packed.reshape(experts, 2, capacity, features)
    primary = packed[:, 0]
    spare_rows = packed[:, 1]
    spare_gate, spare_up, spare_down = (w_gate, w_up, w_down)
    outgoing = jnp.repeat(jnp.stack([primary, spare_rows], axis=1), 2, axis=0)
    arrived = lax.all_to_all(outgoing, "expert", split_axis=0, concat_axis=0, tiled=True)
    sources = arrived.shape[0]
    slot_count = arrived.shape[2]
    first_part = expert_pass(arrived[:, 0].reshape(-1, features), w_gate, w_up, w_down)
    second = expert_pass(arrived[:, 1].reshape(-1, features), spare_gate, spare_up, spare_down)
    partials = jnp.stack(
        [
            first_part.reshape(sources, slot_count, features),
            second.reshape(sources, slot_count, features),
        ],
        axis=1,
    )
    returned = lax.all_to_all(partials, "expert", split_axis=0, concat_axis=0, tiled=True)
    returned = returned.reshape(experts, 2, 2, slot_count, features)
    results = returned[:, 0] + returned[:, 1]
    first_back = results[:, 0]
    second_back = results[:, 1]
    outputs = jnp.stack([first_back, second_back], axis=1).reshape(sections * capacity, features)
    scaled = jnp.sum(jnp.where(matches, gate_weights[None, :, :], 0.0), axis=2)
    combined = jnp.einsum(
        "st,sd->td",
        scaled,
        outputs,
        precision=lax.Precision.HIGHEST,
        preferred_element_type=jnp.float32,
    )
    kept_gate = jnp.where(retained.reshape(tok_rows, chosen), gate_weights, 0.0)
    expert_match = expert_ids[:, :, None] == jnp.arange(experts, dtype=jnp.int32)[None, None, :]
    local_load = jnp.sum(jnp.where(expert_match, kept_gate[:, :, None], 0.0), axis=(0, 1))
    load_sum = lax.psum(local_load, ("dp", "expert"))
    expert_load = load_sum / (tok_rows * lax.axis_size("dp") * members)
    return (combined.astype(jnp.bfloat16), expert_load)


def solution(mesh):
    return jax.shard_map(
        local,
        mesh=mesh,
        in_specs=(
            P(("dp", "expert"), None),
            P(("dp", "expert"), None),
            P(("dp", "expert"), None),
            P(("dp", "expert"), None),
            P(None, "expert"),
            P(None, "expert"),
            P("expert", None),
        ),
        out_specs=(P(("dp", "expert"), None), P()),
        check_vma=False,
    )
```

profile of v0, /device:TPU:1, one launch (start us, length us, event | category | flops | bytes accessed | tf_op | source)
XLA Modules:
  0.0 745.2 jit_solution(16465194769176981721)
XLA Ops:
  0.6 0.8 multiply_add_fusion
  1.5 0.1 copy.38
  1.6 0.1 eq.56
  1.8 0.1 eq.52
  1.9 0.6 reduce-window.6
  2.5 0.2 slice_reduce_fusion
  2.7 0.1 fusion.9
  2.8 0.1 reduce_sum.39
  3.0 0.1 copy.41
  3.1 0.8 convert_reduce_fusion
  3.8 1.5 convolution_convert_fusion
  5.3 0.3 broadcast_in_dim.44
  5.6 220.9 %all_to_all.10 = bf16[32,2,8,2048]{3,2,1,0:T(8,128)(2,1)S(1)} all-to-all(bf16[32,2,8,2048]{3,2,1,0:T(8,128)(2,1)S(1)} %bitcast.54), channel_id=1, replica_groups=mesh['dp'=32,'expert'=32] {'expert'}, dimensions={0} | all-to-all | bytes 4194304 | tf_op jit(solution)/shard_map/all_to_all | solution.py:38
  226.4 1.9 fusion.3
  228.4 1.9 fusion.2
  230.3 5.8 convolution_bitcast_fusion.1
  236.1 5.9 convolution_bitcast_fusion
  242.0 4.6 pad_maximum_fusion
  246.6 16.1 %all-to-all-start.1 = ((f32[32,2,8,2048]{3,2,1,0:T(8,128)}), f32[32,2,8,2048]{3,2,1,0:T(8,128)}, u32[]{:S(2)}, u32[]{:S(2)}) async-start(f32[32,2,8,2048]{3,2,1,0:T(8,128)} %pad_maximum_fusion), calls=%async_computation.1 | async-start | bytes 8388608 | tf_op jit(solution)/shard_map/all_to_all | solution.py:50
  262.8 0.1 select_reduce_fusion.1
  262.9 477.3 %psum.7 = f32[16]{0:T(128)S(1)} all-reduce(f32[16]{0:T(128)S(1)} %select_reduce_fusion.1), channel_id=1, replica_groups=mesh['dp'=32,'expert'=32] {'dp','expert'}, use_global_device_ids=true, to_apply=%region_6.7 | all-reduce | flops 16 | bytes 128 | tf_op jit(solution)/shard_map/psum | solution.py:67
  740.2 0.5 broadcast_multiply_fusion
  740.7 2.5 slice_add_fusion
  743.2 2.0 convolution_convert_fusion.1
  (16 shorter events, 0.1 us)
Async XLA Ops:
  0.6 229.6 %copy-start = (bf16[768,2048]{1,0:T(8,128)(2,1)S(1)}, bf16[768,2048]{1,0:T(8,128)(2,1)}, u32[]{:S(2)}) copy-start(bf16[768,2048]{1,0:T(8,128)(2,1)} %param.13) | copy-start | bytes 9437188
  5.3 221.1 %copy-start.4 = (bf16[2048,768]{1,0:T(8,128)(2,1)S(1)}, bf16[2048,768]{1,0:T(8,128)(2,1)}, u32[]{:S(2)}) copy-start(bf16[2048,768]{1,0:T(8,128)(2,1)} %param.11) | copy-start | bytes 9437188
  226.4 1.9 copy-start.1
  246.6 16.1 %copy-start.2 = (f32[128,2]{0,1:T(2,128)S(1)}, f32[128,2]{0,1:T(2,128)}, u32[]{:S(2)}) copy-start(f32[128,2]{0,1:T(2,128)} %param.10) | copy-start | bytes 3076
  246.6 16.1 %copy-start.3 = (s32[128,2]{0,1:T(2,128)S(1)}, s32[128,2]{0,1:T(2,128)}, u32[]{:S(2)}) copy-start(s32[128,2]{0,1:T(2,128)} %param.8) | copy-start | bytes 3076
  246.6 494.1 %all-to-all-start.1 = ((f32[32,2,8,2048]{3,2,1,0:T(8,128)}), f32[32,2,8,2048]{3,2,1,0:T(8,128)}, u32[]{:S(2)}, u32[]{:S(2)}) async-start(f32[32,2,8,2048]{3,2,1,0:T(8,128)} %pad_maximum_fusion), calls=%async_computation.1 | async-start | bytes 8388608 | tf_op jit(solution)/shard_map/all_to_all | solution.py:50
where the time goes:
time: 746 us; the launch traced here: 745 us
  blocking collectives  698 us (94%)
  matrix products  19 us (3%)
  starting transfers between devices  16.1 us (2%)
  other arithmetic  10.1 us (1%)
    psum x1, blocking collectives, local(): load_sum = lax.psum(local_load, ('dp', 'expert'))  477 us
    all_to_all x1, blocking collectives, local(): lax.all_to_all(outgoing, 'expert', split_axis=0, concat_axis=0, tiled=True)  221 us
    all_to_all x1, starting transfers between devices, local(): lax.all_to_all(partials, 'expert', split_axis=0, concat_axis=0, tiled=True)  16.1 us
  transfers between devices with their start and end apart: 1, of which 0 were waited for; matrix products, arithmetic and copies ran while one was open for 0% of the time, Pallas kernels for 0%

commit v1 on v0

v1 whole, which is shorter than its diff:
```python
import jax
import jax.numpy as jnp
from jax import lax
from jax.experimental import pallas as pl
from jax.experimental.pallas import tpu as pltpu
from jax.sharding import PartitionSpec as P

MESH = pl.DeviceIdType.MESH

BLOCKS = 4
DEPTH = 8
SIDE = 4
PLANE = SIDE * SIDE
CAP = 8
GU_ROWS = 64
DN_ROWS = 32
N_OWN = 8
PEAK = 32


def routing(ids_ref, copy_ref, gate_ref):
    rows = ids_ref.shape[0]
    lanes = lax.broadcasted_iota(jnp.int32, (rows, 128), 1)
    ids = [ids_ref[:, k : k + 1] for k in (0, 1)]
    copies = [copy_ref[:, k : k + 1] for k in (0, 1)]
    hot = [(lanes == 2 * ids[k] + copies[k]).astype(jnp.float32) for k in (0, 1)]
    earlier = lax.broadcasted_iota(jnp.int32, (rows, rows), 1) < lax.broadcasted_iota(
        jnp.int32, (rows, rows), 0
    )
    before = jnp.dot(
        earlier.astype(jnp.float32).astype(jnp.bfloat16),
        (hot[0] + hot[1]).astype(jnp.bfloat16),
        preferred_element_type=jnp.float32,
    )
    ranks = [
        jnp.sum(before * hot[0], axis=1, keepdims=True),
        jnp.sum((before + hot[0]) * hot[1], axis=1, keepdims=True),
    ]
    routes = []
    for k in (0, 1):
        kept = ranks[k] < float(CAP)
        place = (copies[k] * CAP).astype(jnp.float32) + ranks[k]
        gate = jnp.where(kept, gate_ref[:, k : k + 1], 0.0)
        routes.append((ids[k], place, kept, gate))
    return routes


def load_kernel(ids_ref, copy_ref, gate_ref, out_ref):
    lanes = lax.broadcasted_iota(jnp.int32, (ids_ref.shape[0], 128), 1)
    total = jnp.zeros((1, 128), jnp.float32)
    for expert, _, _, gate in routing(ids_ref, copy_ref, gate_ref):
        total += jnp.sum(jnp.where(lanes == expert, gate, 0.0), axis=0, keepdims=True)
    out_ref[...] = jnp.broadcast_to(total, out_ref.shape)


def moe_kernel(
    tokens_ref, ids_ref, copy_ref, gate_ref, wg_ref, wu_ref, wd_ref, out_ref,
    gu, dn, packed, arrived, result, back, acc,
    own_sem, o_send, o_recv, z_send, z_recv, d_send, d_recv, x_send, x_recv, r_send, r_recv,
):
    dp, ex = lax.axis_index("dp"), lax.axis_index("expert")
    zlo, y = dp // SIDE, lax.rem(dp, SIDE)
    x, b, c = ex // (2 * BLOCKS), lax.rem(ex // 2, BLOCKS), lax.rem(ex, 2)
    me = x * SIDE + y
    first_core = c == 0
    features = tokens_ref.shape[1]
    quarter = dn.shape[1]
    gu_chunks = features // GU_ROWS
    chunks = gu_chunks + quarter // DN_ROWS
    own_rows = features // N_OWN
    own_pieces = N_OWN + quarter // 128
    slots = 2 * CAP

    def at_plane(step):
        z = lax.rem(b * DEPTH + zlo + step + BLOCKS * DEPTH, BLOCKS * DEPTH)
        zb, zl = z // DEPTH, lax.rem(z, DEPTH)
        return (zl * SIDE + y, x * 2 * BLOCKS + zb * 2 + c)

    def at_peer(peer):
        return (zlo * SIDE + lax.rem(peer, SIDE), (peer // SIDE) * 2 * BLOCKS + b * 2 + c)

    def peer_of(i):
        return lax.rem(me + i, PLANE)

    ahead = jnp.where(first_core, 1, -1)
    downstream, upstream = at_plane(ahead), at_plane(-ahead)
    partner = (dp, x * 2 * BLOCKS + b * 2 + 1 - c)

    holder = c == y // 2
    column = pl.multiple_of(lax.rem(y, 2) * quarter, 128)

    def own_copies(p):
        if p < N_OWN:
            rows = pl.ds(p * own_rows, own_rows)
            return [
                pltpu.make_async_copy(
                    w.at[rows, pl.ds(column, quarter)],
                    gu.at[0, rows, pl.ds(k * quarter, quarter)],
                    own_sem.at[2 * p + k],
                )
                for k, w in ((0, wg_ref), (1, wu_ref))
            ]
        at = (p - N_OWN) * 128
        return [
            pltpu.make_async_copy(
                wd_ref.at[pl.ds(column + at, 128), :],
                dn.at[0, pl.ds(at, 128), :],
                own_sem.at[N_OWN + p],
            )
        ]

    def own_to_partner(p):
        ref = gu.at[0, pl.ds(p * own_rows, own_rows)] if p < N_OWN else dn.at[0, pl.ds((p - N_OWN) * 128, 128)]
        return pltpu.make_async_remote_copy(
            ref, ref, o_send.at[p], o_recv.at[p], device_id=partner, device_id_type=MESH
        )

    own_order = []
    for p in range((own_pieces + 1) // 2):
        own_order += [p] if p == own_pieces - 1 - p else [p, own_pieces - 1 - p]

    @pl.when(holder)
    def _():
        for p in own_order:
            for copy in own_copies(p):
                copy.start()

    barrier = pltpu.get_barrier_semaphore()

    def greet(i, carry):
        pl.semaphore_signal(barrier, inc=1, device_id=at_peer(peer_of(i)), device_id_type=MESH)
        return carry

    pl.semaphore_signal(barrier, inc=1, device_id=upstream, device_id_type=MESH)
    pl.semaphore_signal(barrier, inc=1, device_id=partner, device_id_type=MESH)
    lax.fori_loop(1, PLANE, greet, 0)

    routes = routing(ids_ref, copy_ref, gate_ref)
    codes = []
    for expert, place, kept, _ in routes:
        group = lax.rem(b - expert + BLOCKS * SIDE, BLOCKS) * SIDE + expert // BLOCKS
        codes.append(jnp.where(kept, (group * slots).astype(jnp.float32) + place, -1.0))
    n_tokens = tokens_ref.shape[0]
    width = BLOCKS * SIDE * slots
    lanes = lax.broadcasted_iota(jnp.int32, (n_tokens, width), 1)
    plain = lanes.astype(jnp.float32)
    select = jnp.where(plain == codes[0], 1.0, 0.0) + jnp.where(plain == codes[1], 1.0, 0.0)
    rows = jnp.dot(
        select.T.astype(jnp.bfloat16), tokens_ref[...], preferred_element_type=jnp.float32
    ).astype(jnp.bfloat16)
    packed[...] = rows.reshape(packed.shape)

    pl.semaphore_wait(barrier, PLANE + 1)

    @pl.when(holder)
    def _():
        for p in own_order:
            for copy in own_copies(p):
                copy.wait()
            own_to_partner(p).start()

    side = jnp.where(first_core, 1, 3)
    other_side = 4 - side
    last = jnp.where(first_core, zlo == DEPTH - 1, zlo == 0)

    def chunk_at(t, mine=True):
        ascending = first_core if mine else jnp.logical_not(first_core)
        return jnp.where(ascending, t, chunks - 1 - t)

    def on_chunk(chunk, act):
        @pl.when(chunk < gu_chunks)
        def _():
            act(lambda s: gu.at[s, pl.ds(pl.multiple_of(chunk * GU_ROWS, GU_ROWS), GU_ROWS)])

        @pl.when(chunk >= gu_chunks)
        def _():
            at = (chunk - gu_chunks) * DN_ROWS
            act(lambda s: dn.at[s, pl.ds(pl.multiple_of(at, DN_ROWS), DN_ROWS)])

    def along(src, dst, sem):
        return pltpu.make_async_remote_copy(
            src, dst, z_send.at[sem], z_recv.at[sem], device_id=downstream, device_id_type=MESH
        )

    def across(ref, sem):
        return pltpu.make_async_remote_copy(
            ref, ref, d_send.at[sem], d_recv.at[sem], device_id=partner, device_id_type=MESH
        )

    def send_own(t, carry):
        on_chunk(chunk_at(t), lambda view: along(view(0), view(side), t).start())
        return carry

    @pl.when(jnp.logical_and(last, holder))
    def _():
        lax.fori_loop(0, chunks, send_own, 0)

    @pl.when(jnp.logical_and(last, jnp.logical_not(holder)))
    def _():
        per_piece = chunks // own_pieces

        @pl.when(first_core)
        def _():
            for i in range(own_pieces):
                own_to_partner(i).wait_recv()
                lax.fori_loop(i * per_piece, (i + 1) * per_piece, send_own, 0)

        @pl.when(jnp.logical_not(first_core))
        def _():
            for i in range(own_pieces):
                own_to_partner(own_pieces - 1 - i).wait_recv()
                lax.fori_loop(i * per_piece, (i + 1) * per_piece, send_own, 0)

    def to_peer(r, peer):
        return pltpu.make_async_remote_copy(
            packed.at[r, peer // SIDE], arrived.at[r, me], x_send.at[r, peer], x_recv.at[r, me],
            device_id=at_peer(peer), device_id_type=MESH,
        )

    def from_peer(r, peer):
        return pltpu.make_async_remote_copy(
            packed.at[r, peer // SIDE], arrived.at[r, peer], x_send.at[r, peer], x_recv.at[r, peer],
            device_id=at_peer(peer), device_id_type=MESH,
        )

    for r in (0, 1, 3, 2):
        lax.fori_loop(1, PLANE, lambda i, s, r=r: (to_peer(r, peer_of(i)).start(), s)[1], 0)
        arrived[r, me] = packed[r, x]

    def home(r, peer):
        return pltpu.make_async_remote_copy(
            result.at[r, peer], back.at[r, me], r_send.at[r, peer], r_recv.at[r, me],
            device_id=at_peer(peer), device_id_type=MESH,
        )

    def from_home(r, peer):
        return pltpu.make_async_remote_copy(
            result.at[r, peer], back.at[r, peer], r_send.at[r, peer], r_recv.at[r, peer],
            device_id=at_peer(peer), device_id_type=MESH,
        )

    def far_count(plane):
        falling = PEAK - ((2 * PEAK - chunks) * plane) // (DEPTH - 1)
        return jnp.where(first_core, falling, chunks - falling)

    far = far_count(zlo)
    far_next = jnp.where(last, PEAK, far_count(zlo + ahead))
    far_partner = chunks - far
    total = chunks + far
    place = jnp.where(first_core, zlo, DEPTH - 1 - zlo)
    early = 14 - 2 * place
    later = 68 - (40 * place) // 7

    def wait_partner(lo, n):
        def one(i, carry):
            on_chunk(chunk_at(i, False), lambda view: across(view(0), lo + i).wait_recv())
            return carry

        lax.fori_loop(0, n, one, 0)

    def step(u, carry):
        @pl.when(u < total)
        def _():
            near = u < chunks
            t = jnp.where(near, u, u - chunks)
            slot = jnp.where(near, side, 2)
            forward = jnp.where(
                last,
                jnp.logical_and(near, t < PEAK),
                jnp.logical_or(near, t < far_next),
            )
            target = jnp.where(last, 2, slot)
            sem = jnp.where(last, chunks + t, u)

            def act(view):
                along(view(0), view(slot), u).wait_recv()

                @pl.when(forward)
                def _():
                    along(view(slot), view(target), sem).start()

                across(view(slot), u).start()

            on_chunk(chunk_at(t), act)

        at_early, at_later, at_near, at_end = u == early, u == later, u == chunks - 1, u == total

        @pl.when(at_early | at_later | at_near | at_end)
        def _():
            r = jnp.where(at_early, 0, jnp.where(at_near, side, jnp.where(at_later, other_side, 2)))

            @pl.when(at_early & jnp.logical_not(holder) & jnp.logical_not(last))
            def _():
                for p in range(own_pieces):
                    own_to_partner(p).wait_recv()

            @pl.when(at_later)
            def _():
                wait_partner(0, chunks)

            @pl.when(at_end)
            def _():
                wait_partner(chunks, far_partner)

            lax.fori_loop(1, PLANE, lambda i, s: (from_peer(r, peer_of(i)).wait_recv(), s)[1], 0)
            inputs = arrived[r].reshape(PLANE * slots, features)
            both = jnp.dot(inputs, gu[r], preferred_element_type=jnp.float32)
            gate_act, up_act = both[:, :quarter], both[:, quarter:]
            hidden = (gate_act / (1.0 + jnp.exp(-gate_act)) * up_act).astype(jnp.bfloat16)
            part = jnp.dot(hidden, dn[r], preferred_element_type=jnp.float32)
            result[r] = part.astype(jnp.bfloat16).reshape(PLANE, slots, features)
            lax.fori_loop(1, PLANE, lambda i, s: (home(r, peer_of(i)).start(), s)[1], 0)
            back[r, me] = result[r, me]

        return carry

    lax.fori_loop(0, total + 1, step, 0)

    lane = lax.broadcasted_iota(jnp.int32, (n_tokens, PLANE * slots), 1)
    code = ((lane // (SIDE * slots)) * slots + lax.rem(lane, slots)).astype(jnp.float32)
    acc[...] = jnp.zeros_like(acc)

    def combine(r):
        lax.fori_loop(1, PLANE, lambda i, s: (from_home(r, peer_of(i)).wait_recv(), s)[1], 0)
        here = code + jnp.float32(r * SIDE * slots)
        scale = jnp.where(here == codes[0], routes[0][3], 0.0) + jnp.where(here == codes[1], routes[1][3], 0.0)
        high = scale.astype(jnp.bfloat16)
        low = (scale - high.astype(jnp.float32)).astype(jnp.bfloat16)
        values = back[r].reshape(PLANE * slots, features)
        acc[...] += jnp.dot(high, values, preferred_element_type=jnp.float32) + jnp.dot(
            low, values, preferred_element_type=jnp.float32
        )

    for r in (0, 1, 3, 2):
        combine(r)
    out_ref[...] = acc[...].astype(out_ref.dtype)

    @pl.when(holder)
    def _():
        for p in range(own_pieces):
            own_to_partner(p).wait_send()

    def sent_along(u, carry):
        on_chunk(
            chunk_at(jnp.where(u < chunks, u, u - chunks)),
            lambda view: along(view(0), view(0), u).wait_send(),
        )
        return carry

    def sent_across(u, carry):
        on_chunk(
            chunk_at(jnp.where(u < chunks, u, u - chunks)),
            lambda view: across(view(0), u).wait_send(),
        )
        return carry

    lax.fori_loop(0, chunks + far_next, sent_along, 0)
    lax.fori_loop(0, total, sent_across, 0)
    for r in range(BLOCKS):
        lax.fori_loop(1, PLANE, lambda i, s, r=r: (to_peer(r, peer_of(i)).wait_send(), s)[1], 0)
        lax.fori_loop(1, PLANE, lambda i, s, r=r: (home(r, peer_of(i)).wait_send(), s)[1], 0)


def local(tokens, expert_ids, copy_choice, gate_weights, w_gate, w_up, w_down):
    n_tokens, features = tokens.shape
    quarter = w_gate.shape[1] // 2
    slots = 2 * CAP
    chunks = features // GU_ROWS + quarter // DN_ROWS
    pieces = N_OWN + quarter // 128
    vmem = pl.BlockSpec(memory_space=pltpu.VMEM)
    anywhere = pl.BlockSpec(memory_space=pl.ANY)
    local_load = pl.pallas_call(
        load_kernel,
        out_shape=jax.ShapeDtypeStruct((8, 128), jnp.float32),
        in_specs=[vmem] * 3,
        out_specs=vmem,
    )(expert_ids, copy_choice, gate_weights)[0, : BLOCKS * SIDE]
    load = lax.psum(local_load, ("dp", "expert")) / (
        n_tokens * lax.axis_size("dp") * lax.axis_size("expert")
    )
    dma = pltpu.SemaphoreType.DMA
    grid_rows = (BLOCKS, PLANE, slots, features)
    out = pl.pallas_call(
        moe_kernel,
        out_shape=jax.ShapeDtypeStruct(tokens.shape, tokens.dtype),
        in_specs=[vmem] * 4 + [anywhere] * 3,
        out_specs=vmem,
        scratch_shapes=[
            pltpu.VMEM((BLOCKS, features, 2 * quarter), jnp.bfloat16),
            pltpu.VMEM((BLOCKS, quarter, features), jnp.bfloat16),
            pltpu.VMEM((BLOCKS, SIDE, slots, features), jnp.bfloat16),
            pltpu.VMEM(grid_rows, jnp.bfloat16),
            pltpu.VMEM(grid_rows, jnp.bfloat16),
            pltpu.VMEM(grid_rows, jnp.bfloat16),
            pltpu.VMEM((n_tokens, features), jnp.float32),
            dma((N_OWN + pieces,)),
            dma((pieces,)),
            dma((pieces,)),
            dma((chunks + PEAK,)),
            dma((chunks + PEAK,)),
            dma((chunks + PEAK,)),
            dma((chunks + PEAK,)),
            dma((BLOCKS, PLANE)),
            dma((BLOCKS, PLANE)),
            dma((BLOCKS, PLANE)),
            dma((BLOCKS, PLANE)),
        ],
        compiler_params=pltpu.CompilerParams(
            collective_id=0, has_side_effects=True, vmem_limit_bytes=56 * 1024 * 1024
        ),
        cost_estimate=pl.CostEstimate(
            flops=5_000_000_000, bytes_accessed=200_000_000, transcendentals=1_000_000
        ),
    )(tokens, expert_ids, copy_choice, gate_weights, w_gate, w_up, w_down)
    return out, load


def solution(mesh):
    return jax.shard_map(
        local,
        mesh=mesh,
        in_specs=(
            P(("dp", "expert"), None),
            P(("dp", "expert"), None),
            P(("dp", "expert"), None),
            P(("dp", "expert"), None),
            P(None, "expert"),
            P(None, "expert"),
            P("expert", None),
        ),
        out_specs=(P(("dp", "expert"), None), P()),
        check_vma=False,
    )
```

time: 746 us -> 329 us (0.44)
  blocking collectives: 698 us -> 170 us
  Pallas kernels: 0 us -> 146 us
  matrix products: 19 us -> 0 us
  starting transfers between devices: 16.1 us -> 0 us
  other arithmetic: 10.1 us -> 0.51 us
    psum x1, blocking collectives: 477 us -> 170 us  [local(): lax.psum(local_load, ('dp', 'expert'))]
    all_to_all x1 -> x0, blocking collectives: 221 us -> none  [local(): lax.all_to_all(outgoing, 'expert', split_axis=0, concat_axis=0, tiled=True)]
    pallas_call x0 -> x2, Pallas kernels: none -> 146 us  [the longest x1 144 us: local(): pl.pallas_call(moe_kernel, out_shape=jax.ShapeDtypeStruct(tokens.shape, t...]
    dot_general x6 -> x0, matrix products: 19 us -> none  [the longest x2 11.7 us: expert_pass(): return jnp.dot(hidden, weight_down, preferred_element_type=jnp.float32)]
    all_to_all x1 -> x0, starting transfers between devices: 16.1 us -> none  [local(): lax.all_to_all(partials, 'expert', split_axis=0, concat_axis=0, tiled=True)]
  transfers between devices with their start and end apart: 1 -> 0, of which waited for: 0 -> 0; matrix products, arithmetic and copies ran while one was open for 0% -> 0% of each run, Pallas kernels for 0% -> 0%
where the time goes in v1:
time: 329 us; the launch traced here: 325 us
  blocking collectives  170 us (52%)
  Pallas kernels  146 us (44%)
  local copies, waits for them, and re-layouts  6.78 us (2%)
    psum x1, blocking collectives, local(): lax.psum(local_load, ('dp', 'expert'))  170 us
    pallas_call x1, Pallas kernels, local(): pl.pallas_call(moe_kernel, out_shape=jax.ShapeDtypeStruct(tokens.shape, t...  144 us

profile of v1, /device:TPU:1, one launch (start us, length us, event | category | flops | bytes accessed | tf_op | source)
XLA Modules:
  0.0 324.5 jit_solution(8243645220155351801)
XLA Ops:
  0.6 1.4 copy.9.ids_ref
  2.0 1.4 copy.10.copy_ref
  3.4 1.4 copy.11.gate_ref
  4.8 1.9 shard_map.87
  6.8 0.7 slice_bitcast_fusion
  7.5 170.4 %psum.7 = f32[16]{0:T(128)S(1)} all-reduce(f32[16]{0:T(128)S(1)} %slice_bitcast_fusion), channel_id=1, replica_groups=mesh['dp'=32,'expert'=32] {'dp','expert'}, use_global_device_ids=true, to_apply=%region_0.0 | all-reduce | flops 16 | bytes 128 | tf_op jit(solution)/shard_map/psum | solution.py:378
  177.8 0.5 broadcast_multiply_fusion
  178.3 144.3 %shard_map.86 = bf16[128,2048]{1,0:T(8,128)(2,1)} custom-call(bf16[128,2048]{1,0:T(8,128)(2,1)} %tokens_ref.1, s32[128,2]{1,0:T(8,128)} %copy.9.ids_ref, s32[128,2]{1,0:T(8,128)} %copy.10.copy_ref, f32[128,2]{1,0:T(8,128)} %copy.11.gate_ref, bf16[2048,768]{1,0:T(8,128)(2,1)} %wg_ref.1, bf16[2048,768]{1,0:T(8,128)(2,1)} %wu_ref.1, bf16[768,2048]{1,0:T(8,128)(2,1)} %wd_ref.1), custom_call_target="tpu_custom_call" | custom-call | flops 5000000000 | bytes 200000000 | tf_op jit(solution)/shard_map/pallas_call | solution.py:383
  322.6 1.9 copy.16

commit v2 on v1

--- a/solution.py
+++ b/solution.py
@@ -15,14 +15,15 @@
 GU_ROWS = 64
 DN_ROWS = 32
 N_OWN = 8
+REACH = 4
 PEAK = 32
 
 
-def routing(ids_ref, copy_ref, gate_ref):
-    rows = ids_ref.shape[0]
+def routing(columns):
+    rows = columns.shape[0]
     lanes = lax.broadcasted_iota(jnp.int32, (rows, 128), 1)
-    ids = [ids_ref[:, k : k + 1] for k in (0, 1)]
-    copies = [copy_ref[:, k : k + 1] for k in (0, 1)]
+    ids = [columns[:, k : k + 1].astype(jnp.int32) for k in (0, 1)]
+    copies = [columns[:, k + 2 : k + 3].astype(jnp.int32) for k in (0, 1)]
     hot = [(lanes == 2 * ids[k] + copies[k]).astype(jnp.float32) for k in (0, 1)]
     earlier = lax.broadcasted_iota(jnp.int32, (rows, rows), 1) < lax.broadcasted_iota(
         jnp.int32, (rows, rows), 0
@@ -40,23 +41,16 @@
     for k in (0, 1):
         kept = ranks[k] < float(CAP)
         place = (copies[k] * CAP).astype(jnp.float32) + ranks[k]
-        gate = jnp.where(kept, gate_ref[:, k : k + 1], 0.0)
+        gate = jnp.where(kept, columns[:, k + 4 : k + 5], 0.0)
         routes.append((ids[k], place, kept, gate))
     return routes
 
 
-def load_kernel(ids_ref, copy_ref, gate_ref, out_ref):
-    lanes = lax.broadcasted_iota(jnp.int32, (ids_ref.shape[0], 128), 1)
-    total = jnp.zeros((1, 128), jnp.float32)
-    for expert, _, _, gate in routing(ids_ref, copy_ref, gate_ref):
-        total += jnp.sum(jnp.where(lanes == expert, gate, 0.0), axis=0, keepdims=True)
-    out_ref[...] = jnp.broadcast_to(total, out_ref.shape)
-
-
 def moe_kernel(
-    tokens_ref, ids_ref, copy_ref, gate_ref, wg_ref, wu_ref, wd_ref, out_ref,
-    gu, dn, packed, arrived, result, back, acc,
+    tokens_ref, ids_ref, copy_ref, gate_ref, wg_ref, wu_ref, wd_ref, out_ref, load_ref,
+    gu, dn, packed, arrived, result, back, acc, square, core_loads, chip_loads, plane_loads, other_loads, all_loads,
     own_sem, o_send, o_recv, z_send, z_recv, d_send, d_recv, x_send, x_recv, r_send, r_recv,
+    c_send, c_recv, p_send, p_recv, l_send, l_recv, m_send, m_recv,
 ):
     dp, ex = lax.axis_index("dp"), lax.axis_index("expert")
     zlo, y = dp // SIDE, lax.rem(dp, SIDE)
@@ -83,7 +77,7 @@
         return lax.rem(me + i, PLANE)
 
     ahead = jnp.where(first_core, 1, -1)
-    downstream, upstream = at_plane(ahead), at_plane(-ahead)
+    downstream = at_plane(ahead)
     partner = (dp, x * 2 * BLOCKS + b * 2 + 1 - c)
 
     holder = c == y // 2
@@ -131,11 +125,16 @@
         pl.semaphore_signal(barrier, inc=1, device_id=at_peer(peer_of(i)), device_id_type=MESH)
         return carry
 
-    pl.semaphore_signal(barrier, inc=1, device_id=upstream, device_id_type=MESH)
+    for d in range(1, REACH + 1):
+        pl.semaphore_signal(barrier, inc=1, device_id=at_plane(-d * ahead), device_id_type=MESH)
     pl.semaphore_signal(barrier, inc=1, device_id=partner, device_id_type=MESH)
     lax.fori_loop(1, PLANE, greet, 0)
 
-    routes = routing(ids_ref, copy_ref, gate_ref)
+    square[...] = jnp.zeros_like(square)
+    square[0:2, :] = ids_ref[...].astype(jnp.float32)
+    square[2:4, :] = copy_ref[...].astype(jnp.float32)
+    square[4:6, :] = gate_ref[...]
+    routes = routing(square[...].T)
     codes = []
     for expert, place, kept, _ in routes:
         group = lax.rem(b - expert + BLOCKS * SIDE, BLOCKS) * SIDE + expert // BLOCKS
@@ -149,8 +148,30 @@
         select.T.astype(jnp.bfloat16), tokens_ref[...], preferred_element_type=jnp.float32
     ).astype(jnp.bfloat16)
     packed[...] = rows.reshape(packed.shape)
-
-    pl.semaphore_wait(barrier, PLANE + 1)
+    experts = lax.broadcasted_iota(jnp.int32, (n_tokens, 128), 1)
+    load = jnp.zeros((1, 128), jnp.float32)
+    for expert, _, _, gate in routes:
+        load += jnp.sum(jnp.where(experts == expert, gate, 0.0), axis=0, keepdims=True)
+    core_loads[0] = jnp.broadcast_to(load, core_loads.shape[1:])
+
+    pl.semaphore_wait(barrier, PLANE + REACH)
+
+    core_load = pltpu.make_async_remote_copy(
+        core_loads.at[0], core_loads.at[1], c_send, c_recv, device_id=partner, device_id_type=MESH
+    )
+    core_load.start()
+
+    def load_to(peer):
+        return pltpu.make_async_remote_copy(
+            chip_loads.at[me], chip_loads.at[me], p_send.at[peer], p_recv.at[me],
+            device_id=at_peer(peer), device_id_type=MESH,
+        )
+
+    def load_from(peer):
+        return pltpu.make_async_remote_copy(
+            chip_loads.at[peer], chip_loads.at[peer], p_send.at[peer], p_recv.at[peer],
+            device_id=at_peer(peer), device_id_type=MESH,
+        )
 
     @pl.when(holder)
     def _():
@@ -211,6 +232,10 @@
                 own_to_partner(own_pieces - 1 - i).wait_recv()
                 lax.fori_loop(i * per_piece, (i + 1) * per_piece, send_own, 0)
 
+    core_load.wait_recv()
+    chip_loads[me] = core_loads[0] + core_loads[1]
+    lax.fori_loop(1, PLANE, lambda i, s: (load_to(peer_of(i)).start(), s)[1], 0)
+
     def to_peer(r, peer):
         return pltpu.make_async_remote_copy(
             packed.at[r, peer // SIDE], arrived.at[r, me], x_send.at[r, peer], x_recv.at[r, me],
@@ -242,14 +267,52 @@
     def far_count(plane):
         falling = PEAK - ((2 * PEAK - chunks) * plane) // (DEPTH - 1)
         return jnp.where(first_core, falling, chunks - falling)
+
+    planes = BLOCKS * DEPTH
+    rounds = planes // 2 // REACH
+    z_here = b * DEPTH + zlo
+    lax.fori_loop(1, PLANE, lambda i, s: (load_from(peer_of(i)).wait_recv(), s)[1], 0)
+    plane_loads[0] = jnp.sum(chip_loads[...], axis=0)
+
+    def load_first(d):
+        return pltpu.make_async_remote_copy(
+            plane_loads.at[0], plane_loads.at[d], l_send.at[d - 1], l_recv.at[d - 1],
+            device_id=at_plane(d * ahead), device_id_type=MESH,
+        )
+
+    def load_on(k):
+        return pltpu.make_async_remote_copy(
+            plane_loads.at[pl.ds((k - 1) * REACH + 1, REACH)], plane_loads.at[pl.ds(k * REACH + 1, REACH)],
+            l_send.at[REACH + k - 1], l_recv.at[REACH + k - 1],
+            device_id=at_plane(REACH * ahead), device_id_type=MESH,
+        )
+
+    def load_across(k):
+        return pltpu.make_async_remote_copy(
+            plane_loads.at[pl.ds(k * REACH + 1, REACH)], other_loads.at[pl.ds(k * REACH + 1, REACH)],
+            m_send.at[k], m_recv.at[k], device_id=partner, device_id_type=MESH,
+        )
+
+    for d in range(1, REACH + 1):
+        load_first(d).start()
+
+    def load_round(k):
+        if k == 1:
+            for d in range(1, REACH + 1):
+                load_first(d).wait_recv()
+        else:
+            load_on(k - 1).wait_recv()
+        load_across(k - 1).start()
+        if k < rounds:
+            load_on(k).start()
 
     far = far_count(zlo)
     far_next = jnp.where(last, PEAK, far_count(zlo + ahead))
     far_partner = chunks - far
     total = chunks + far
     place = jnp.where(first_core, zlo, DEPTH - 1 - zlo)
-    early = 14 - 2 * place
-    later = 68 - (40 * place) // 7
+    early = 24 - 2 * place
+    later = 74 - (40 * place) // 7
 
     def wait_partner(lo, n):
         def one(i, carry):
@@ -258,7 +321,15 @@
 
         lax.fori_loop(0, n, one, 0)
 
+    shift = (20 * place) // 7
+
     def step(u, carry):
+        for k, when in ((1, 20), (2, 40), (3, 58)):
+
+            @pl.when(u == when - shift)
+            def _(k=k):
+                load_round(k)
+
         @pl.when(u < total)
         def _():
             near = u < chunks
@@ -316,6 +387,16 @@
 
     lax.fori_loop(0, total + 1, step, 0)
 
+    load_round(rounds)
+    for k in range(rounds):
+        load_across(k).wait_recv()
+    for k in range(planes // 2 + 1):
+        all_loads[lax.rem(z_here - k * ahead + planes, planes)] = plane_loads[k]
+    for k in range(1, planes // 2):
+        all_loads[lax.rem(z_here + k * ahead + planes, planes)] = other_loads[k]
+    tokens_in_all = n_tokens * lax.axis_size("dp") * lax.axis_size("expert")
+    load_ref[...] = jnp.sum(all_loads[...], axis=0) * (1.0 / tokens_in_all)
+
     lane = lax.broadcasted_iota(jnp.int32, (n_tokens, PLANE * slots), 1)
     code = ((lane // (SIDE * slots)) * slots + lax.rem(lane, slots)).astype(jnp.float32)
     acc[...] = jnp.zeros_like(acc)
@@ -335,6 +416,15 @@
         combine(r)
     out_ref[...] = acc[...].astype(out_ref.dtype)
 
+    core_load.wait_send()
+    lax.fori_loop(1, PLANE, lambda i, s: (load_to(peer_of(i)).wait_send(), s)[1], 0)
+    for d in range(1, REACH + 1):
+        load_first(d).wait_send()
+    for k in range(1, rounds):
+        load_on(k).wait_send()
+    for k in range(rounds):
+        load_across(k).wait_send()
+
     @pl.when(holder)
     def _():
         for p in range(own_pieces):
@@ -369,22 +459,16 @@
     pieces = N_OWN + quarter // 128
     vmem = pl.BlockSpec(memory_space=pltpu.VMEM)
     anywhere = pl.BlockSpec(memory_space=pl.ANY)
-    local_load = pl.pallas_call(
-        load_kernel,
-        out_shape=jax.ShapeDtypeStruct((8, 128), jnp.float32),
-        in_specs=[vmem] * 3,
-        out_specs=vmem,
-    )(expert_ids, copy_choice, gate_weights)[0, : BLOCKS * SIDE]
-    load = lax.psum(local_load, ("dp", "expert")) / (
-        n_tokens * lax.axis_size("dp") * lax.axis_size("expert")
-    )
     dma = pltpu.SemaphoreType.DMA
     grid_rows = (BLOCKS, PLANE, slots, features)
-    out = pl.pallas_call(
+    out, load = pl.pallas_call(
         moe_kernel,
-        out_shape=jax.ShapeDtypeStruct(tokens.shape, tokens.dtype),
+        out_shape=[
+            jax.ShapeDtypeStruct(tokens.shape, tokens.dtype),
+            jax.ShapeDtypeStruct((8, 128), jnp.float32),
+        ],
         in_specs=[vmem] * 4 + [anywhere] * 3,
-        out_specs=vmem,
+        out_specs=[vmem] * 2,
         scratch_shapes=[
             pltpu.VMEM((BLOCKS, features, 2 * quarter), jnp.bfloat16),
             pltpu.VMEM((BLOCKS, quarter, features), jnp.bfloat16),
@@ -393,6 +477,12 @@
             pltpu.VMEM(grid_rows, jnp.bfloat16),
             pltpu.VMEM(grid_rows, jnp.bfloat16),
             pltpu.VMEM((n_tokens, features), jnp.float32),
+            pltpu.VMEM((n_tokens, 128), jnp.float32),
+            pltpu.VMEM((2, 8, 128), jnp.float32),
+            pltpu.VMEM((PLANE, 8, 128), jnp.float32),
+            pltpu.VMEM((BLOCKS * DEPTH // 2 + 1, 8, 128), jnp.float32),
+            pltpu.VMEM((BLOCKS * DEPTH // 2 + 1, 8, 128), jnp.float32),
+            pltpu.VMEM((BLOCKS * DEPTH, 8, 128), jnp.float32),
             dma((N_OWN + pieces,)),
             dma((pieces,)),
             dma((pieces,)),
@@ -404,6 +494,14 @@
             dma((BLOCKS, PLANE)),
             dma((BLOCKS, PLANE)),
             dma((BLOCKS, PLANE)),
+            dma,
+            dma,
+            dma((PLANE,)),
+            dma((PLANE,)),
+            dma((2 * REACH,)),
+            dma((2 * REACH,)),
+            dma((REACH,)),
+            dma((REACH,)),
         ],
         compiler_params=pltpu.CompilerParams(
             collective_id=0, has_side_effects=True, vmem_limit_bytes=56 * 1024 * 1024
@@ -411,8 +509,8 @@
         cost_estimate=pl.CostEstimate(
             flops=5_000_000_000, bytes_accessed=200_000_000, transcendentals=1_000_000
         ),
-    )(tokens, expert_ids, copy_choice, gate_weights, w_gate, w_up, w_down)
-    return out, load
+    )(tokens, expert_ids.T, copy_choice.T, gate_weights.T, w_gate, w_up, w_down)
+    return out, load[0, : BLOCKS * SIDE]
 
 
 def solution(mesh):

time: 329 us -> 182 us (0.55)
  the two profiles are of different devices: /device:TPU:1 before, /device:TPU:249 now
where the time goes in v2:
time: 182 us
  Pallas kernels  178 us (98%)
  local copies, waits for them, and re-layouts  3.07 us (2%)
    pallas_call x1, Pallas kernels, local(): pl.pallas_call(moe_kernel, out_shape=[jax.ShapeDtypeStruct(tokens.shape,...  178 us

profile of v2, /device:TPU:249, one launch (start us, length us, event | category | flops | bytes accessed | tf_op | source)
XLA Modules:
  0.0 182.0 jit_solution(11466084129208777250)
XLA Ops:
  0.6 178.3 %shard_map.86 = (bf16[128,2048]{1,0:T(8,128)(2,1)}, f32[8,128]{1,0:T(8,128)}) custom-call(bf16[128,2048]{1,0:T(8,128)(2,1)} %tokens_ref.1, s32[2,128]{1,0:T(2,128)} %bitcast.5, s32[2,128]{1,0:T(2,128)} %bitcast.6, f32[2,128]{1,0:T(2,128)} %bitcast.7, bf16[2048,768]{1,0:T(8,128)(2,1)} %wg_ref.1, bf16[2048,768]{1,0:T(8,128)(2,1)} %wu_ref.1, ...), custom_call_target="tpu_custom_call" | custom-call | flops 5000000000 | bytes 200000000 | tf_op jit(solution)/shard_map/pallas_call | solution.py:464
  178.9 1.2 slice_bitcast_fusion
  180.1 1.9 %copy.10 = bf16[128,2048]{1,0:T(8,128)(2,1)} copy(bf16[128,2048]{1,0:T(8,128)(2,1)} %get-tuple-element.8) | data formatting | bytes 1048576
